TPU v7x, 128 devices: a whole 4x4x4 slice. The times are simulated.
128 devices in a mesh: row: 8 (over x, core), col: 16 (over z, y).
Axes of the slice: x: 4, y: 4, z: 4, core: 2. Of those that a mesh axis runs over, the one named last changes fastest.
Arguments:
- diag_inverse: bfloat16 [2048, 2048], P(('row', 'col')), as said below
- row_left: bfloat16 [8, 2048, 256], P('row', 'col'), may hold values from -3 to 3
- row_right: bfloat16 [8, 2048, 256], P('row', 'col'), may hold values from -0.125 to 0.125
- col_left: bfloat16 [64, 2048, 256], P('col', 'row'), may hold values from -3 to 3
- col_right: bfloat16 [64, 2048, 256], P('col', 'row'), may hold values from -0.125 to 0.125
- row_ranks: int32 [8], P('row'), may hold values from 32 to 256, as said below
- col_ranks: int32 [64], P('col'), may hold values from 32 to 256, as said below
- tile_left: bfloat16 [8, 64, 2048, 256], P('row', 'col'), may hold values from -0.125 to 0.125
- tile_right: bfloat16 [8, 64, 2048, 256], P('row', 'col'), may hold values from -6 to 6
- new_ranks: int32 [8, 64], P('row', 'col'), may hold values from 32 to 256, as said below
Outputs:
- updated: bfloat16 [8, 64, 2048, 256], P('row', 'col')
Inputs may be any that keep to these rules, and one draw needn't show every extreme that they name: diag_inverse is lower triangular with diagonal entries between 0.5 and 1.5. `row_ranks`: some panel tile has rank 256 and some has rank 256 // 8. `col_ranks`: some panel tile has rank 256 and some has rank 256 // 8. `new_ranks`: some tile keeps rank 256 and some keeps 256 // 8.
All inputs are finite; a program needn't handle non-finite values.
Results may differ from a plain program's by a relative error of at most 0.0067.
Values may be sent and summed in bfloat16 or wider, within the bound.
A program may use at most 128 MiB of HBM per device.

v0:
```python
import jax
import jax.numpy as jnp
from jax import lax
from jax.sharding import PartitionSpec as P


def keep_columns(ranks, rank_width):
    columns = lax.broadcasted_iota(jnp.int32, ranks.shape + (rank_width,), ranks.ndim)
    return columns < ranks[..., None]


def upper_block(left_tile, right_tile, left_panel, combined_block, rank, offset, width):
    columns = left_tile[:, offset : offset + width]
    keep = (lax.broadcasted_iota(jnp.int32, (width,), 0) + offset < rank).astype(jnp.float32)
    gram_block = (
        jnp.einsum("nr,ns->rs", left_tile, columns, preferred_element_type=jnp.float32)
        * keep[None, :]
    ).astype(jnp.bfloat16)
    first_term = jnp.dot(right_tile, gram_block, preferred_element_type=jnp.float32)
    second_term = jnp.dot(left_panel, combined_block, preferred_element_type=jnp.float32)
    return (first_term - second_term).astype(jnp.bfloat16)


def on_device(
    diag_inverse,
    row_left,
    row_right,
    col_left,
    col_right,
    row_ranks,
    col_ranks,
    tile_left,
    tile_right,
    new_ranks,
):
    rank_width = row_right.shape[2]
    row_right = row_right * keep_columns(row_ranks, rank_width)[:, None, :].astype(jnp.bfloat16)
    col_right = col_right * keep_columns(col_ranks, rank_width)[:, None, :].astype(jnp.bfloat16)
    row_left_full, row_right_full = (
        lax.all_gather(row_left, "col", axis=1, tiled=True),
        lax.all_gather(row_right, "col", axis=1, tiled=True),
    )
    col_left_full, col_right_full = (
        lax.all_gather(col_left, "row", axis=1, tiled=True),
        lax.all_gather(col_right, "row", axis=1, tiled=True),
    )
    row_count = row_right_full.shape[0]
    tile_width = row_right_full.shape[1]
    stacked = jnp.concatenate((row_right_full, col_right_full), 0)
    solved = jnp.einsum(
        "nm,tmr->tnr",
        lax.all_gather(diag_inverse, ("row", "col"), axis=0, tiled=True),
        stacked,
        preferred_element_type=jnp.float32,
    ).astype(jnp.bfloat16)
    solved_rows = solved[:row_count]
    solved_cols = solved[row_count:]
    coupling = jnp.einsum(
        "inr,jns->ijrs", solved_rows, solved_cols, preferred_element_type=jnp.float32
    ).astype(jnp.bfloat16)
    retained = keep_columns(new_ranks, rank_width).astype(jnp.float32)[:, :, None, :]
    projected = (
        jnp.einsum("inr,ijns->ijrs", row_left_full, tile_left, preferred_element_type=jnp.float32)
        * retained
    ).astype(jnp.bfloat16)
    combined = jnp.einsum(
        "ijab,ijac->ijbc", coupling, projected, preferred_element_type=jnp.float32
    ).astype(jnp.bfloat16)
    half_width = rank_width // 2
    keep_lower = keep_columns(new_ranks, half_width).astype(jnp.float32)[:, :, None, :]
    gram_lower = (
        jnp.einsum(
            "ijnr,ijns->ijrs",
            tile_left,
            tile_left[:, :, :, :half_width],
            preferred_element_type=jnp.float32,
        )
        * keep_lower
    ).astype(jnp.bfloat16)
    first_lower = jnp.einsum(
        "ijnr,ijrs->ijns", tile_right, gram_lower, preferred_element_type=jnp.float32
    )
    second_lower = jnp.einsum(
        "jnb,ijbc->ijnc",
        col_left_full,
        combined[:, :, :, :half_width],
        preferred_element_type=jnp.float32,
    )
    lower_out = (first_lower - second_lower).astype(jnp.bfloat16)
    tile_rows = tile_left.shape[0]
    tile_cols = tile_left.shape[1]
    unit_count = tile_rows * tile_cols
    left_flat = tile_left.reshape(unit_count, tile_width, rank_width)
    right_flat = tile_right.reshape(unit_count, tile_width, rank_width)
    combined_upper = combined.reshape(unit_count, rank_width, rank_width)[:, :, half_width:]
    ranks_flat = new_ranks.reshape(unit_count)
    column_of = jnp.arange(unit_count, dtype=jnp.int32) % tile_cols
    live = ranks_flat > half_width
    empty_block = jnp.zeros((tile_width, half_width), jnp.bfloat16)

    def owned_block(operands):
        left_tile, right_tile, combined_block, rank, column, active = operands
        return lax.cond(
            active,
            lambda: upper_block(
                left_tile,
                right_tile,
                col_left_full[column],
                combined_block,
                rank,
                half_width,
                half_width,
            ),
            lambda: empty_block,
        )

    upper_out = lax.map(
        owned_block, (left_flat, right_flat, combined_upper, ranks_flat, column_of, live)
    )
    upper_out = upper_out.reshape(tile_rows, tile_cols, tile_width, half_width)
    return jnp.concatenate((lower_out, upper_out), 3)


def solution(mesh):
    in_specs = (
        P(("row", "col"), None),
        P("row", "col", None),
        P("row", "col", None),
        P("col", "row", None),
        P("col", "row", None),
        P("row"),
        P("col"),
        P("row", "col", None, None),
        P("row", "col", None, None),
        P("row", "col"),
    )
    out_specs = P("row", "col", None, None)
    return jax.shard_map(
        on_device, mesh=mesh, in_specs=in_specs, out_specs=out_specs, check_vma=False
    )
```

profile of v0, /device:TPU:5, one launch (start us, length us, event | category | flops | bytes accessed | tf_op | source)
XLA Modules:
  0.0 306.4 jit_solution(8399942501616225497)
XLA Ops:
  6.5 0.7 all-gather.12.cloned.1.call-update
  7.3 0.9 copy.11
  8.9 0.7 broadcast_multiply_fusion.1
  9.7 1.2 copy.12
  11.0 0.7 fusion.46
  11.7 1.0 broadcast_multiply_fusion
  12.8 0.5 all-gather.10.cloned.1.call-update
  13.4 0.5 all-gather.14.cloned.1.call-update
  13.9 0.7 broadcast_compare_fusion
  14.6 0.7 fusion.48
  15.3 0.7 fusion.47
  16.0 8.3 %fusion.42 = f32[4,128,2048]{2,1,0:T(8,128)} fusion(bf16[1,4,2048,256]{3,2,1,0:T(8,128)(2,1)} %param.21, f32[4,128]{1,0:T(4,128)S(1)} %fusion.48, bf16[1,4,2048,256]{3,2,1,0:T(8,128)(2,1)} %param.22), kind=kOutput, calls=%fused_computation.44 | convolution fusion | flops 1074003968 | bytes 14682112 | tf_op jit(solution)/shard_map/ijnr,ijrs->ijns/dot_general | solution.py:80
  24.3 29.0 %all-gather.12.cloned.1.call-done = bf16[1,2048,256]{2,1,0:T(8,128)(2,1)} async-done(((bf16[1,128,256]{2,1,0:T(8,128)(2,1)}), bf16[1,2048,256]{2,1,0:T(8,128)(2,1)}) %all-gather.12.cloned.1.call-update) | async-done | bytes 1048592 | tf_op jit(solution)/shard_map/all_gather | solution.py:40
  53.3 3.8 %fusion.34 = bf16[4,256,256]{1,2,0:T(8,128)(2,1)S(1)} fusion(bf16[1,2048,256]{2,1,0:T(8,128)(2,1)} %all-gather.12.cloned.1.call-done, f32[4,256]{1,0:T(4,128)S(1)} %fusion.47, bf16[1,4,2048,256]{3,2,1,0:T(8,128)(2,1)} %param.21), kind=kOutput, calls=%fused_computation.41 | convolution fusion | flops 1074266112 | bytes 5771264 | tf_op jit(solution)/shard_map/inr,ijns->ijrs/dot_general | solution.py:63
  57.1 41.2 %all-gather.6.cloned.1.call-done = bf16[1,2048,256]{1,2,0:T(8,128)(2,1)} async-done(((bf16[1,128,256]{1,2,0:T(8,128)(2,1)}), bf16[1,2048,256]{1,2,0:T(8,128)(2,1)}) %all-gather.6.cloned.1.call-update) | async-done | bytes 1048592 | tf_op jit(solution)/shard_map/all_gather | solution.py:41
  98.3 38.5 %all-gather.8.cloned.1.call-done = bf16[4,2048,256]{1,2,0:T(8,128)(2,1)} async-done(((bf16[4,256,256]{1,2,0:T(8,128)(2,1)}), bf16[4,2048,256]{1,2,0:T(8,128)(2,1)}) %all-gather.8.cloned.1.call-update) | async-done | bytes 4194320 | tf_op jit(solution)/shard_map/all_gather | solution.py:45
  136.7 72.9 %all-gather.10.cloned.1.call-done = bf16[2048,2048]{1,0:T(8,128)(2,1)} async-done(((bf16[16,2048]{1,0:T(8,128)(2,1)}), bf16[2048,2048]{1,0:T(8,128)(2,1)}) %all-gather.10.cloned.1.call-update) | async-done | bytes 8388624 | tf_op jit(solution)/shard_map/all_gather | solution.py:52
  209.7 16.6 %convert_bitcast_fusion = bf16[5,2048,256]{1,2,0:T(8,128)(2,1)} fusion(bf16[2048,2048]{1,0:T(8,128)(2,1)} %all-gather.10.cloned.1.call-done, bf16[4,2048,256]{1,2,0:T(8,128)(2,1)} %all-gather.8.cloned.1.call-done, bf16[1,2048,256]{1,2,0:T(8,128)(2,1)} %all-gather.6.cloned.1.call-done), kind=kOutput, calls=%fused_computation.28 | convolution fusion | flops 10742661120 | bytes 18874368 | tf_op jit(solution)/shard_map/nm,tmr->tnr/dot_general | solution.py:50
  226.2 4.1 %convolution_convert_fusion.1 = bf16[4,256,256]{2,1,0:T(8,128)(2,1)S(1)} fusion(bf16[4,256,256]{1,2,0:T(8,128)(2,1)S(1)} %fusion.34, bf16[5,2048,256]{1,2,0:T(8,128)(2,1)} %convert_bitcast_fusion), kind=kOutput, calls=%fused_computation.39 | convolution fusion | flops 1208483840 | bytes 7340032 | tf_op jit(solution)/shard_map/ijab,ijac->ijbc/dot_general | solution.py:66
  230.5 10.6 %all-gather.14.cloned.1.call-done = bf16[4,2048,256]{2,1,0:T(8,128)(2,1)} async-done(((bf16[4,256,256]{2,1,0:T(8,128)(2,1)}), bf16[4,2048,256]{2,1,0:T(8,128)(2,1)}) %all-gather.14.cloned.1.call-update) | async-done | bytes 4194320 | tf_op jit(solution)/shard_map/all_gather | solution.py:44
  241.0 45.0 %while.11 = (s32[]{:T(128)}, bf16[4,2048,128]{1,2,0:T(8,128)(2,1)}, pred[4]{0:T(512)(128)(4,1)S(1)}, bf16[4,2048,256]{2,1,0:T(8,128)(2,1)}, bf16[4,2048,256]{2,1...) while((s32[]{:T(128)}, bf16[4,2048,128]{1,2,0:T(8,128)(2,1)}, ...), condition=%wide.region_3.4_spmd.clone, body=%wide.region_0.3_spmd.clone.sunk | while | flops 403243424 | bytes 10554266 | solution.py:117
  241.0 0.6 dynamic_slice.69
  242.3 8.9 %conditional.3 = (bf16[1,2048,128]{2,1,0:T(8,128)(2,1)S(1)}) conditional(s32[]{:T(128)} %bitcast.101, () %tuple.39, (bf16[4,2048,256]{2,1,0:T(8,128)(2,1)}, s32[]{:T(128)}, bf16[4,2048,256]{2,1,0:T(8,128)(2,1)}, s32[4]{0:T(128)S(1)}, s32[4]{0:T(128)S(1)}, /*index=5*/bf16[4,2048,256]{2,1,0:T(8,128)(2,1)}, bf16[4,256,128]{2,1,0:T(8,128)(2,1)S(1)}, ...), branch_computations={%region_1.1_spmd, %region_2.2_spmd.clone} | conditional | flops 403243424 | bytes 8456366 | solution.py:103
  242.3 0.6 dynamic_slice.52
  244.9 1.3 dynamic-slice_bitcast_fusion
  246.2 0.6 dynamic_slice.51
  246.8 0.6 compare_convert_fusion
  247.4 2.1 fusion.5
  249.5 1.7 fusion.3
  251.2 0.2 copy.27
  251.4 0.9 constant_dynamic-update-slice_fusion.2
  252.3 0.6 dynamic_slice.69
  253.6 8.9 %conditional.3 = (bf16[1,2048,128]{2,1,0:T(8,128)(2,1)S(1)}) conditional(s32[]{:T(128)} %bitcast.101, () %tuple.39, (bf16[4,2048,256]{2,1,0:T(8,128)(2,1)}, s32[]{:T(128)}, bf16[4,2048,256]{2,1,0:T(8,128)(2,1)}, s32[4]{0:T(128)S(1)}, s32[4]{0:T(128)S(1)}, /*index=5*/bf16[4,2048,256]{2,1,0:T(8,128)(2,1)}, bf16[4,256,128]{2,1,0:T(8,128)(2,1)S(1)}, ...), branch_computations={%region_1.1_spmd, %region_2.2_spmd.clone} | conditional | flops 403243424 | bytes 8456366 | solution.py:103
  253.6 0.6 dynamic_slice.52
  256.1 1.3 dynamic-slice_bitcast_fusion
  257.4 0.6 dynamic_slice.51
  258.1 0.6 compare_convert_fusion
  258.7 2.1 fusion.5
  260.8 1.7 fusion.3
  262.5 0.2 copy.27
  262.7 0.8 constant_dynamic-update-slice_fusion.2
  263.5 0.6 dynamic_slice.69
  264.8 8.9 %conditional.3 = (bf16[1,2048,128]{2,1,0:T(8,128)(2,1)S(1)}) conditional(s32[]{:T(128)} %bitcast.101, () %tuple.39, (bf16[4,2048,256]{2,1,0:T(8,128)(2,1)}, s32[]{:T(128)}, bf16[4,2048,256]{2,1,0:T(8,128)(2,1)}, s32[4]{0:T(128)S(1)}, s32[4]{0:T(128)S(1)}, /*index=5*/bf16[4,2048,256]{2,1,0:T(8,128)(2,1)}, bf16[4,256,128]{2,1,0:T(8,128)(2,1)S(1)}, ...), branch_computations={%region_1.1_spmd, %region_2.2_spmd.clone} | conditional | flops 403243424 | bytes 8456366 | solution.py:103
  264.9 0.6 dynamic_slice.52
  267.4 1.3 dynamic-slice_bitcast_fusion
  268.7 0.6 dynamic_slice.51
  269.3 0.6 compare_convert_fusion
  269.9 2.1 fusion.5
  272.0 1.7 fusion.3
  273.7 0.2 copy.27
  273.9 0.8 constant_dynamic-update-slice_fusion.2
  274.8 0.6 dynamic_slice.69
  276.0 8.9 %conditional.3 = (bf16[1,2048,128]{2,1,0:T(8,128)(2,1)S(1)}) conditional(s32[]{:T(128)} %bitcast.101, () %tuple.39, (bf16[4,2048,256]{2,1,0:T(8,128)(2,1)}, s32[]{:T(128)}, bf16[4,2048,256]{2,1,0:T(8,128)(2,1)}, s32[4]{0:T(128)S(1)}, s32[4]{0:T(128)S(1)}, /*index=5*/bf16[4,2048,256]{2,1,0:T(8,128)(2,1)}, bf16[4,256,128]{2,1,0:T(8,128)(2,1)S(1)}, ...), branch_computations={%region_1.1_spmd, %region_2.2_spmd.clone} | conditional | flops 403243424 | bytes 8456366 | solution.py:103
  276.1 0.6 dynamic_slice.52
  278.6 1.3 dynamic-slice_bitcast_fusion
  279.9 0.6 dynamic_slice.51
  280.5 0.6 compare_convert_fusion
  281.2 2.1 fusion.5
  283.3 1.7 fusion.3
  284.9 0.2 copy.27
  285.2 0.8 constant_dynamic-update-slice_fusion.2
  286.0 5.1 %fusion.23 = bf16[1,4,2048,128]{2,3,1,0:T(8,128)(2,1)S(1)} fusion(f32[4,128,2048]{2,1,0:T(8,128)} %fusion.42, bf16[4,2048,256]{2,1,0:T(8,128)(2,1)} %get-tuple-element.286, bf16[1,4,256,256]{3,2,1,0:T(8,128)(2,1)S(1)} %bitcast.106), kind=kOutput, calls=%fused_computation.31 | convolution fusion | flops 538968064 | bytes 10747904 | tf_op jit(solution)/shard_map/jnb,ijbc->ijnc/dot_general | solution.py:83
  291.1 2.5 pad_maximum_fusion
  293.6 6.2 %copy.18 = bf16[1,4,2048,256]{3,2,1,0:T(8,128)(2,1)} copy(bf16[1,4,2048,256]{2,3,1,0:T(8,128)(2,1)} %pad_maximum_fusion) | data formatting | bytes 8388608 | tf_op jit(solution)/shard_map/concatenate | solution.py:121
  (26 shorter events, 0.3 us)
Async XLA Ops:
  6.5 46.8 %all-gather.12.cloned.1.call-start = ((), (), s32[]{:S(2)}) async-start(), calls=%async_computation.3 | async-start | bytes 1114112 | tf_op jit(solution)/shard_map/all_gather | solution.py:40
  7.3 91.0 %all-gather.6.cloned.1.call-start = ((), (), s32[]{:S(2)}) async-start(), calls=%async_computation | async-start | bytes 1114112 | tf_op jit(solution)/shard_map/all_gather | solution.py:41
  9.7 127.1 %all-gather.8.cloned.1.call-start = ((), (), s32[]{:S(2)}) async-start(), calls=%async_computation.1 | async-start | bytes 4718592 | tf_op jit(solution)/shard_map/all_gather | solution.py:45
  12.7 196.9 %all-gather.10.cloned.1.call-start = ((), (), s32[]{:S(2)}) async-start(), calls=%async_computation.2 | async-start | bytes 8454144 | tf_op jit(solution)/shard_map/all_gather | solution.py:52
  13.3 227.7 %all-gather.14.cloned.1.call-start = ((), (), s32[]{:S(2)}) async-start(), calls=%async_computation.4 | async-start | bytes 4718592 | tf_op jit(solution)/shard_map/all_gather | solution.py:44
  226.2 14.8 %copy-start.1 = (s32[1,4]{1,0:T(1,128)S(1)}, s32[1,4]{1,0:T(1,128)}, u32[]{:S(2)}) copy-start(s32[1,4]{1,0:T(1,128)} %param.23) | copy-start | bytes 52
  286.0 5.1 %copy-start = (bf16[4,2048,128]{1,2,0:T(8,128)(2,1)S(1)}, bf16[4,2048,128]{1,2,0:T(8,128)(2,1)}, u32[]{:S(2)}) copy-start(bf16[4,2048,128]{1,2,0:T(8,128)(2,1)} %get-tuple-element.130) | copy-start | bytes 6291460
Sparse Core Ops, SparseCore 0:
  9.5 43.7 all-gather.11
  55.4 42.8 all-gather.5
  99.9 36.7 all-gather.7
  139.7 69.8 all-gather.9
  211.2 29.7 all-gather.13
where the time goes:
time: 307 us; the launch traced here: 306 us
  waiting for transfers between devices  194 us (63%)
  matrix products  52.9 us (17%)
  local copies, waits for them, and re-layouts  25.6 us (8%)
  between operations  13.9 us (5%)
  loops' own time  10.2 us (3%)
  other arithmetic  9.66 us (3%)
    all_gather x1, waiting for transfers between devices, on_device(): lax.all_gather(diag_inverse, ('row', 'col'), axis=0, tiled=True)  72.9 us
    all_gather x1, waiting for transfers between devices, on_device(): lax.all_gather(row_right, 'col', axis=1, tiled=True)  41.2 us
    all_gather x1, waiting for transfers between devices, on_device(): lax.all_gather(col_right, 'row', axis=1, tiled=True)  38.5 us
    all_gather x1, waiting for transfers between devices, on_device(): lax.all_gather(row_left, 'col', axis=1, tiled=True)  29 us
    dot_general x1, matrix products, on_device(): jnp.einsum('nm,tmr->tnr', lax.all_gather(diag_inverse, ('row', 'col'), ax...  16.6 us
    all_gather x1, waiting for transfers between devices, on_device(): lax.all_gather(col_left, 'row', axis=1, tiled=True)  10.6 us
    dot_general x4, matrix products, upper_block(): jnp.dot(right_tile, gram_block, preferred_element_type=jnp.float32)  8.37 us
    dot_general x1, matrix products, on_device(): jnp.einsum('ijnr,ijrs->ijns', tile_right, gram_lower, preferred_element_t...  8.26 us
  transfers between devices with their start and end apart: 5, of which 5 were waited for; matrix products, arithmetic and copies ran while one was open for 13% of the time, Pallas kernels for 0%

commit v1 on v0

v1 whole, which is shorter than its diff:
```python
import functools

import jax
import jax.numpy as jnp
from jax import lax
from jax.experimental import pallas as pl
from jax.experimental.pallas import tpu as pltpu
from jax.sharding import PartitionSpec as P

MESH = pl.DeviceIdType.MESH
F32 = jnp.float32
BF16 = jnp.bfloat16

OWN_AHEAD, OWN_BACK, OWN_SIB, PASS_AHEAD, BACK_SIB, AHEAD_SIB, FAR_SIB = range(7)


def dot(a, b):
    return jnp.dot(a, b, preferred_element_type=F32)


def tdot(a, b):
    return lax.dot_general(a, b, (((0,), (0,)), ((), ())), preferred_element_type=F32)


def kernel(
    row_ranks,
    col_ranks,
    new_ranks,
    diag,
    row_left,
    row_right,
    col_left,
    col_right,
    tile_left,
    tile_right,
    out,
    tl,
    tr,
    cr,
    cl,
    rl,
    xr,
    sv,
    yv,
    dr,
    dc,
    gram,
    proj,
    comb,
    res,
    load_sem,
    out_sem,
    x_send,
    x_recv,
    d_send,
    d_recv,
    a_send,
    a_recv,
    g_send,
    g_recv,
):
    r = lax.axis_index("row")
    c = lax.axis_index("col")
    x, k = r // 2, r % 2
    z, y = c // 4, c % 4
    step = 1 - 2 * k
    ahead_x = (x + step + 4) % 4
    back_x = (x - step + 4) % 4
    far_x = (x + 2) % 4
    sib = (2 * x + 1 - k, c)
    ahead = (2 * ahead_x + k, c)
    back = (2 * back_x + k, c)
    far = (2 * far_x + k, c)
    pending = []

    def send(src, dst, ssem, rsem, device):
        copy = pltpu.make_async_remote_copy(
            src_ref=src, dst_ref=dst, send_sem=ssem, recv_sem=rsem, device_id=device, device_id_type=MESH
        )
        copy.start()
        return copy

    barrier = pltpu.get_barrier_semaphore()
    for device in (ahead, back, far, sib):
        pl.semaphore_signal(barrier, inc=1, device_id=device, device_id_type=MESH)
    for d in range(1, 16):
        pl.semaphore_signal(barrier, inc=1, device_id=(r, (c + d) % 16), device_id_type=MESH)

    def load(src, dst, n):
        copy = pltpu.make_async_copy(src, dst, load_sem.at[n])
        copy.start()
        return copy

    load_d = load(diag, dr.at[x, k], 0)
    load_x = load(row_right.at[0], xr.at[z, y], 1)
    load_l = load(row_left.at[0], rl.at[z, y], 2)
    load_tl = [load(tile_left.at[0, j], tl.at[j], 3 + j) for j in range(4)]
    load_cr = load(col_right, cr.at[r], 7)
    load_cl = load(col_left, cl.at[r], 8)
    load_tr = load(tile_right.at[0], tr, 9)
    pl.semaphore_wait(barrier, 19)

    def gather_first(n, src, buf):
        copies = []
        for d in range(1, 4):
            for h, device in ((0, (r, 4 * z + (y + d) % 4)), (1, (r, 4 * ((z + d) % 4) + y))):
                rows = pl.ds(64 * h, 64)
                s = 6 * h + d - 1
                copies.append(
                    send(src.at[rows], buf.at[z, y, rows], g_send.at[n, s], g_recv.at[n, s], device)
                )
        pending.extend(copies)
        return copies

    def gather_second(n, buf, firsts):
        for copy in firsts:
            copy.wait_recv()
        copies = []
        for d in range(1, 4):
            part = buf.at[z, :, pl.ds(0, 64)]
            copies.append(send(part, part, g_send.at[n, 2 + d], g_recv.at[n, 2 + d], (r, 4 * ((z + d) % 4) + y)))
            part = buf.at[:, y, pl.ds(64, 64)]
            copies.append(send(part, part, g_send.at[n, 8 + d], g_recv.at[n, 8 + d], (r, 4 * z + (y + d) % 4)))
        pending.extend(copies)
        return copies

    def wait_all(copies):
        for copy in copies:
            copy.wait_recv()

    panels = (cr, cl)

    def panel_copy(kind, t, j, slot, device):
        ref = panels[t].at[slot, j]
        s = 4 * t + j
        return pltpu.make_async_remote_copy(
            src_ref=ref, dst_ref=ref, send_sem=x_send.at[kind, s], recv_sem=x_recv.at[kind, s],
            device_id=device, device_id_type=MESH,
        )

    def panel_own(t, j):
        panel_copy(OWN_AHEAD, t, j, r, ahead).start()
        panel_copy(OWN_BACK, t, j, r, back).start()
        panel_copy(OWN_SIB, t, j, r, sib).start()

    back_slot = 2 * back_x + k
    ahead_slot = 2 * ahead_x + k
    far_slot = 2 * far_x + k

    def panel_pass(t, j):
        panel_copy(OWN_AHEAD, t, j, back_slot, ahead).wait_recv()
        panel_copy(PASS_AHEAD, t, j, back_slot, ahead).start()
        panel_copy(BACK_SIB, t, j, back_slot, sib).start()
        panel_copy(OWN_BACK, t, j, ahead_slot, back).wait_recv()
        panel_copy(AHEAD_SIB, t, j, ahead_slot, sib).start()

    def panel_far(t, j):
        panel_copy(PASS_AHEAD, t, j, far_slot, ahead).wait_recv()
        panel_copy(FAR_SIB, t, j, far_slot, sib).start()

    d_own = [
        send(diag, dr.at[x, k], d_send.at[n], d_recv.at[n], device) for n, device in enumerate((ahead, back, far))
    ]
    pending.extend(d_own)
    x_first = gather_first(0, row_right.at[0], xr)
    load_cr.wait()
    for j in range(4):
        panel_own(0, j)
    load_cl.wait()
    panel_own(1, 0)
    l_first = gather_first(1, row_left.at[0], rl)

    def local_products(j):
        load_tl[j].wait()
        g = tdot(tl[j], tl[j])
        keep = lax.broadcasted_iota(jnp.int32, (256, 256), 1) < new_ranks[0, j]
        gram[j] = jnp.where(keep, g, 0.0).astype(BF16)

    load_x.wait()
    x_second = gather_second(0, xr, x_first)

    load_d.wait()
    wait_all(d_own)
    share = dr.at[:, k]
    d_share = send(share, share, d_send.at[3], d_recv.at[3], sib)
    pending.append(d_share)
    local_products(0)
    d_share.wait_recv()
    half = pl.ds(2 * k, 2)
    for d in range(1, 16):
        dest = (c + d) % 16
        pending.append(
            send(
                dr.at[half, :, :, pl.ds(pl.multiple_of(dest * 128, 128), 128)],
                dc.at[c, half],
                a_send.at[d],
                a_recv.at[d],
                (r, dest),
            )
        )
    a_copies = pending[-15:]
    d_local = load(dr.at[half, :, :, pl.ds(pl.multiple_of(c * 128, 128), 128)], dc.at[c, half], 0)
    local_products(1)

    wait_all(x_second)
    solved = jnp.zeros((128, 256), F32)
    for m in range(8):
        a = dr[:, :, :, 256 * m : 256 * m + 256].reshape(128, 256)
        solved += dot(a, xr[m // 2, 2 * (m % 2) : 2 * (m % 2) + 2].reshape(256, 256))
    sv[z, y] = solved.astype(BF16)
    s_first = gather_first(2, sv.at[z, y], sv)
    load_l.wait()
    l_second = gather_second(1, rl, l_first)
    for j in range(2):
        panel_pass(0, j)
        panel_own(1, j + 1)
    wait_all(a_copies)
    d_local.wait()
    share = dc.at[:, half]
    c_share = send(share, share, a_send.at[0], a_recv.at[0], sib)
    pending.append(c_share)
    s_second = gather_second(2, sv, s_first)
    local_products(2)
    panel_pass(0, 2)
    panel_own(1, 3)
    panel_pass(0, 3)
    local_products(3)
    c_share.wait_recv()

    wait_all(s_second)
    yslab = jnp.zeros((128, 256), F32)
    for m in range(8):
        a = dc[2 * m : 2 * m + 2].reshape(256, 128)
        yslab += tdot(a, sv[m // 2, 2 * (m % 2) : 2 * (m % 2) + 2].reshape(256, 256))
    yv[z, y] = yslab.astype(BF16)
    y_first = gather_first(3, yv.at[z, y], yv)
    wait_all(l_second)

    def projected(j):
        p = jnp.zeros((256, 256), F32)
        for m in range(8):
            a = rl[m // 2, 2 * (m % 2) : 2 * (m % 2) + 2].reshape(256, 256)
            p += tdot(a, tl[j, 256 * m : 256 * m + 256])
        proj[j] = p.astype(BF16)

    projected(0)
    y_second = gather_second(3, yv, y_first)
    for j in range(1, 4):
        projected(j)
    for j in range(4):
        panel_pass(1, j)
    for j in range(4):
        panel_far(0, j)
    for j in range(4):
        for kind, slot in ((OWN_SIB, r), (BACK_SIB, r), (AHEAD_SIB, r), (FAR_SIB, r)):
            panel_copy(kind, 0, j, slot, sib).wait_recv()

    wait_all(y_second)
    for j in range(4):
        g = jnp.zeros((256, 256), F32)
        for m in range(8):
            a = yv[m // 2, 2 * (m % 2) : 2 * (m % 2) + 2].reshape(256, 256)
            g += tdot(a, cr[m, j])
        keep = (lax.broadcasted_iota(jnp.int32, (256, 256), 0) < row_ranks[0]) & (
            lax.broadcasted_iota(jnp.int32, (256, 256), 1) < col_ranks[j]
        )
        coupling = jnp.where(keep, g, 0.0).astype(BF16)
        cm = tdot(coupling, proj[j])
        keep = lax.broadcasted_iota(jnp.int32, (256, 256), 1) < new_ranks[0, j]
        comb[j] = jnp.where(keep, cm, 0.0).astype(BF16)

    def out_copy(slot, j):
        rows = pl.ds(pl.multiple_of(slot * 256, 256), 256)
        return pltpu.make_async_copy(res.at[j, rows], out.at[0, j, rows], out_sem.at[slot, j])

    def update(slot, j):
        rows = pl.ds(pl.multiple_of(slot * 256, 256), 256)
        res[j, rows, :] = (dot(tr[j, rows, :], gram[j]) - dot(cl[slot, j], comb[j])).astype(BF16)
        out_copy(slot, j).start()

    load_tr.wait()
    sib_slot = 2 * x + 1 - k
    sib_back_slot = 2 * ahead_x + 1 - k
    sib_ahead_slot = 2 * back_x + 1 - k
    sib_far_slot = 2 * far_x + 1 - k
    for slot in (r, back_slot, ahead_slot):
        for j in range(4):
            update(slot, j)
    for kind, slot in ((OWN_SIB, sib_slot), (BACK_SIB, sib_back_slot), (AHEAD_SIB, sib_ahead_slot)):
        for j in range(4):
            panel_copy(kind, 1, j, r, sib).wait_recv()
            update(slot, j)
    for j in range(4):
        panel_far(1, j)
        update(far_slot, j)
        panel_copy(FAR_SIB, 1, j, r, sib).wait_recv()
        update(sib_far_slot, j)

    for copy in pending:
        copy.wait_send()
    for t in range(2):
        for j in range(4):
            for kind in range(7):
                panel_copy(kind, t, j, r, sib).wait_send()
    for slot in range(8):
        for j in range(4):
            out_copy(slot, j).wait()


def on_device(
    diag_inverse, row_left, row_right, col_left, col_right, row_ranks, col_ranks, tile_left, tile_right, new_ranks
):
    hbm = pl.BlockSpec(memory_space=pl.ANY)
    smem = pl.BlockSpec(memory_space=pltpu.SMEM)
    dma = pltpu.SemaphoreType.DMA
    return pl.pallas_call(
        kernel,
        out_shape=jax.ShapeDtypeStruct(tile_right.shape, tile_right.dtype),
        in_specs=[smem] * 3 + [hbm] * 7,
        out_specs=hbm,
        scratch_shapes=[
            pltpu.VMEM((4, 2048, 256), BF16),
            pltpu.VMEM((4, 2048, 256), BF16),
            pltpu.VMEM((8, 4, 256, 256), BF16),
            pltpu.VMEM((8, 4, 256, 256), BF16),
            pltpu.VMEM((4, 4, 128, 256), BF16),
            pltpu.VMEM((4, 4, 128, 256), BF16),
            pltpu.VMEM((4, 4, 128, 256), BF16),
            pltpu.VMEM((4, 4, 128, 256), BF16),
            pltpu.VMEM((4, 2, 16, 2048), BF16),
            pltpu.VMEM((16, 4, 2, 16, 128), BF16),
            pltpu.VMEM((4, 256, 256), BF16),
            pltpu.VMEM((4, 256, 256), BF16),
            pltpu.VMEM((4, 256, 256), BF16),
            pltpu.VMEM((4, 2048, 256), BF16),
            dma((10,)),
            dma((8, 4)),
            dma((7, 8)),
            dma((7, 8)),
            dma((4,)),
            dma((4,)),
            dma((16,)),
            dma((16,)),
            dma((4, 12)),
            dma((4, 12)),
        ],
        compiler_params=pltpu.CompilerParams(
            collective_id=0, has_side_effects=True, vmem_limit_bytes=60 * 1024 * 1024
        ),
        name="panel_step",
    )(
        row_ranks, col_ranks, new_ranks, diag_inverse, row_left, row_right, col_left, col_right, tile_left, tile_right
    )


def solution(mesh):
    in_specs = (
        P(("row", "col"), None),
        P("row", "col", None),
        P("row", "col", None),
        P("col", "row", None),
        P("col", "row", None),
        P("row"),
        P("col"),
        P("row", "col", None, None),
        P("row", "col", None, None),
        P("row", "col"),
    )
    out_specs = P("row", "col", None, None)
    return jax.shard_map(on_device, mesh=mesh, in_specs=in_specs, out_specs=out_specs, check_vma=False)
```

time: 307 us -> 68.1 us (0.22)
  the two profiles are of different devices: /device:TPU:5 before, /device:TPU:1 now
where the time goes in v1:
time: 68.1 us; the launch traced here: 67.9 us
  Pallas kernels  62.8 us (92%)
  local copies, waits for them, and re-layouts  4.47 us (7%)
    pallas_call x1, Pallas kernels, on_device(): pl.pallas_call(kernel, out_shape=jax.ShapeDtypeStruct(tile_right.shape, t...  62.8 us
    unnamed x1, local copies, waits for them, and re-layouts  4.47 us

profile of v1, /device:TPU:1, one launch (start us, length us, event | category | flops | bytes accessed | tf_op | source)
XLA Modules:
  0.0 67.9 jit_solution(9874286363829625150)
XLA Ops:
  0.7 62.8 %panel_step.1 = bf16[1,4,2048,256]{3,2,1,0:T(8,128)(2,1)} custom-call(s32[1]{0:T(128)S(6)} %copy.12.row_ranks, s32[4]{0:T(128)} %col_ranks.1, s32[1,4]{1,0:T(1,128)} %new_ranks.1, bf16[16,2048]{1,0:T(8,128)(2,1)} %diag.1, bf16[1,128,256]{2,1,0:T(8,128)(2,1)} %row_left.1, bf16[1,128,256]{2,1,0:T(8,128)(2,1)} %row_right.1, bf16[4,256,256]{2,1,0:T(8,128)(2,1)} %col_left.1, ...), custom_call_target="tpu_custom_call" | custom-call | tf_op jit(solution)/shard_map/panel_step/pallas_call | solution.py:316
  63.4 4.5 %copy.13 = bf16[1,4,2048,256]{3,2,1,0:T(8,128)(2,1)} copy(bf16[1,4,2048,256]{3,2,1,0:T(8,128)(2,1)} %panel_step.1) | data formatting | bytes 8388608

commit v2 on v1

v2 whole, which is shorter than its diff:
```python
import functools

import jax
import jax.numpy as jnp
from jax import lax
from jax.experimental import pallas as pl
from jax.experimental.pallas import tpu as pltpu
from jax.sharding import PartitionSpec as P

MESH = pl.DeviceIdType.MESH
F32 = jnp.float32
BF16 = jnp.bfloat16

OWN_AHEAD, OWN_BACK, OWN_SIB, PASS_AHEAD, BACK_SIB, AHEAD_SIB, FAR_SIB = range(7)


def dot(a, b):
    return jnp.dot(a, b, preferred_element_type=F32)


def tdot(a, b):
    return lax.dot_general(a, b, (((0,), (0,)), ((), ())), preferred_element_type=F32)


def remote(group, src, dst, ssem, rsem, device):
    return pltpu.make_async_remote_copy(
        src_ref=src, dst_ref=dst, send_sem=ssem, recv_sem=rsem, device_id=device, device_id_type=MESH
    )


def kernel(
    row_ranks,
    col_ranks,
    new_ranks,
    diag,
    row_left,
    row_right,
    col_left,
    col_right,
    tile_left,
    tile_right,
    out,
    tl,
    tr,
    cr,
    cl,
    rl,
    xr,
    yacc,
    yt,
    dm,
    gram,
    coup,
    comb,
    term,
    rank_c,
    rank_n,
    load_sem,
    x_send,
    x_recv,
    d_send,
    d_recv,
    a_send,
    a_recv,
    g_send,
    g_recv,
):
    r = lax.axis_index("row")
    c = lax.axis_index("col")
    x, k = r // 2, r % 2
    z, y = c // 4, c % 4
    step = 1 - 2 * k
    ahead_x = (x + step + 4) % 4
    back_x = (x - step + 4) % 4
    far_x = (x + 2) % 4
    sib = (2 * x + 1 - k, c)
    ahead = (2 * ahead_x + k, c)
    back = (2 * back_x + k, c)
    far = (2 * far_x + k, c)
    pending = []

    def send(group, src, dst, ssem, rsem, device):
        copy = remote(group, src, dst, ssem, rsem, device)
        copy.start()
        return copy

    barrier = pltpu.get_barrier_semaphore()
    for device in (ahead, back, far, sib):
        pl.semaphore_signal(barrier, inc=1, device_id=device, device_id_type=MESH)
    for d in range(1, 4):
        for device in ((r, 4 * z + (y + d) % 4), (r, 4 * ((z + d) % 4) + y)):
            pl.semaphore_signal(barrier, inc=1, device_id=device, device_id_type=MESH)

    def load(src, dst, n):
        copy = pltpu.make_async_copy(src, dst, load_sem.at[n])
        copy.start()
        return copy

    load_ranks = [load(col_ranks, rank_c, 10), load(new_ranks, rank_n, 11)]
    load_x = load(row_right.at[0], xr.at[z, y], 1)
    load_d = load(diag, dm.at[x, k, z, y], 0)
    load_tl = [load(tile_left.at[0, j], tl.at[j], 3 + j) for j in range(4)]
    load_l = load(row_left.at[0], rl.at[z, y], 2)
    load_cr = load(col_right, cr.at[:, r], 7)
    load_cl = load(col_left, cl.at[:, 0, k], 8)
    load_tr = load(tile_right.at[0], tr, 9)
    pl.semaphore_wait(barrier, 10)

    def gather_first(n, sources, view):
        copies = []
        for d in range(1, 4):
            for h, device in ((0, (r, 4 * z + (y + d) % 4)), (1, (r, 4 * ((z + d) % 4) + y))):
                s = 3 * h + d - 1
                copies.append(send("gather", sources[h], view(h, z, y), g_send.at[n, s], g_recv.at[n, s], device))
        pending.extend(copies)
        return copies

    def gather_second(n, view, firsts):
        wait_all(firsts)
        halves = []
        for e, d in ((0, 1), (1, 3)):
            for half in (e, 1 - e):
                pair = pl.ds(2 * half, 2)
                for h, device in ((0, (r, 4 * ((z + d) % 4) + y)), (1, (r, 4 * z + (y + d) % 4))):
                    part = view(0, z, pair) if h == 0 else view(1, pair, y)
                    s = 6 + 4 * h + 2 * e + half
                    copy = send("gather", part, part, g_send.at[n, s], g_recv.at[n, s], device)
                    halves.append((copy, h, e, d, half))
                    pending.append(copy)
        return halves

    def gather_relay(n, view, halves):
        copies = []
        for copy, h, e, d, half in halves:
            if half != e:
                copies.append(copy)
                continue
            copy.wait_recv()
            pair = pl.ds(2 * half, 2)
            if h == 0:
                part, device = view(0, (z - d + 4) % 4, pair), (r, 4 * ((z + d) % 4) + y)
            else:
                part, device = view(1, pair, (y - d + 4) % 4), (r, 4 * z + (y + d) % 4)
            s = 14 + 2 * h + e
            relayed = send("gather", part, part, g_send.at[n, s], g_recv.at[n, s], device)
            copies.append(relayed)
            pending.append(relayed)
        return copies

    def wait_all(copies):
        for copy in copies:
            copy.wait_recv()

    def slab_view(buf):
        return lambda h, zz, yy: buf.at[zz, yy, pl.ds(64 * h, 64)]

    def diag_view(p):
        width = 256 * (p + 1)
        return lambda h, zz, yy: dm.at[p, k, zz, yy, :, pl.ds(width * h, width)]

    back_slot = 2 * back_x + k
    ahead_slot = 2 * ahead_x + k
    far_slot = 2 * far_x + k

    def panel_copy(kind, t, j):
        if t == 0:
            slot = {PASS_AHEAD: back_slot, BACK_SIB: back_slot, AHEAD_SIB: ahead_slot, FAR_SIB: far_slot}.get(kind, r)
            src = dst = cr.at[j, slot]
        else:
            here = {PASS_AHEAD: 2 - k, BACK_SIB: 2 - k, AHEAD_SIB: 1 + k, FAR_SIB: 3}.get(kind, 0)
            there = {OWN_AHEAD: 2 - k, OWN_BACK: 1 + k, PASS_AHEAD: 3}.get(kind, here)
            src, dst = cl.at[j, here, k], cl.at[j, there, k]
        device = {OWN_AHEAD: ahead, PASS_AHEAD: ahead, OWN_BACK: back}.get(kind, sib)
        s = 4 * t + j
        return remote("panel", src, dst, x_send.at[kind, s], x_recv.at[kind, s], device)

    def panel_own(t, j):
        for kind in (OWN_AHEAD, OWN_BACK, OWN_SIB):
            panel_copy(kind, t, j).start()

    def panel_pass(t, j):
        panel_copy(OWN_AHEAD, t, j).wait_recv()
        panel_copy(PASS_AHEAD, t, j).start()
        panel_copy(BACK_SIB, t, j).start()
        panel_copy(OWN_BACK, t, j).wait_recv()
        panel_copy(AHEAD_SIB, t, j).start()

    def panel_far(t, j):
        panel_copy(PASS_AHEAD, t, j).wait_recv()
        panel_copy(FAR_SIB, t, j).start()

    def panel_sibling(t, j, kinds):
        for kind in kinds:
            panel_copy(kind, t, j).wait_recv()

    for p in range(4):

        @pl.when(x == p)
        def _():
            for n, device in enumerate((ahead, back, far)):
                part = pl.ds(0, 512 * (p + 1))
                send("diag", diag.at[:, part], dm.at[p, k, z, y, :, part], d_send.at[n], d_recv.at[p], device)

    x_view, l_view = slab_view(xr), slab_view(rl)
    d_view = [diag_view(p) for p in range(4)]
    x_first = gather_first(0, [row_right.at[0, pl.ds(64 * h, 64)] for h in range(2)], x_view)
    l_first = gather_first(1, [row_left.at[0, pl.ds(64 * h, 64)] for h in range(2)], l_view)
    load_cr.wait()
    load_cl.wait()
    for j in range(4):
        panel_own(0, j)
    for j in range(4):
        panel_own(1, j)

    def local_products(j):
        load_tl[j].wait()
        g = tdot(tl[j], tl[j])
        keep = lax.broadcasted_iota(jnp.int32, (256, 256), 1) < rank_n[0, j]
        gram[j] = jnp.where(keep, g, 0.0).astype(BF16)

    def diag_share(p):
        wait_all(d_relay[p])
        part = dm.at[p, k, :, :, :, pl.ds(0, 512 * (p + 1))]
        copy = send("diag", part, part, a_send.at[p], a_recv.at[p], sib)
        pending.append(copy)
        return copy

    def solve(p):
        width = 512 * (p + 1)
        a = dm[p, :, :, :, :, 0:width].reshape(512, width)
        solved = dot(a, xr[0 : p + 1].reshape(width, 256)).astype(BF16).T
        for b in range(p + 1):
            cols = slice(512 * b, 512 * b + 512)
            acc = dot(solved, dm[p, :, :, :, :, cols].reshape(512, 512))
            if p < 3:
                acc += yacc[:, cols]
            if b == p:
                yt[:, cols] = acc.astype(BF16)
            else:
                yacc[:, cols] = acc

    chips = (x, (x + 1) % 4, (x + 3) % 4, far_x)

    def chip_rows(i):
        return pl.ds(pl.multiple_of(chips[i] * 512, 512), 512)

    def first_term(j):
        for i in range(4):
            term[j, i] = dot(tr[j, chip_rows(i), :], gram[j])

    for copy in load_ranks:
        copy.wait()
    local_products(0)
    load_x.wait()
    x_second = gather_second(0, x_view, x_first)
    load_d.wait()
    d_first, d_second, d_relay = {}, {}, {}
    for p in (3, 2, 1, 0):

        @pl.when(x != p)
        def _():
            part = dm.at[p, k, z, y, :, pl.ds(0, 512 * (p + 1))]
            remote("diag", part, part, d_send.at[0], d_recv.at[p], far).wait_recv()

        d_first[p] = gather_first(2 + p, [d_view[p](h, z, y) for h in range(2)], d_view[p])
    local_products(1)
    panel_pass(0, 0)
    local_products(2)
    x_relay = gather_relay(0, x_view, x_second)
    panel_pass(0, 1)
    local_products(3)
    for p in (3, 2, 1, 0):
        d_second[p] = gather_second(2 + p, d_view[p], d_first[p])
    load_tr.wait()
    first_term(0)
    panel_pass(0, 2)
    first_term(1)
    first_term(2)
    panel_pass(0, 3)
    first_term(3)
    wait_all(x_relay)
    panel_pass(1, 0)
    d_relay[3] = gather_relay(5, d_view[3], d_second[3])
    panel_pass(1, 1)
    for p in (2, 1, 0):
        d_relay[p] = gather_relay(2 + p, d_view[p], d_second[p])
    load_l.wait()
    l_second = gather_second(1, l_view, l_first)
    panel_pass(1, 2)
    shares = {3: diag_share(3)}
    panel_pass(1, 3)
    shares[2] = diag_share(2)
    shares[3].wait_recv()
    solve(3)
    shares.update({p: diag_share(p) for p in (1, 0)})
    shares[2].wait_recv()
    solve(2)
    l_relay = gather_relay(1, l_view, l_second)
    for p in (1, 0):
        shares[p].wait_recv()
        solve(p)
    for j in range(4):
        panel_far(0, j)

    for j in range(4):
        panel_sibling(0, j, (OWN_SIB, BACK_SIB, AHEAD_SIB, FAR_SIB))
        g = dot(yt[...], cr[j].reshape(2048, 256))
        keep = (lax.broadcasted_iota(jnp.int32, (256, 256), 0) < row_ranks[0]) & (
            lax.broadcasted_iota(jnp.int32, (256, 256), 1) < rank_c[j]
        )
        coup[j] = jnp.where(keep, g, 0.0).astype(BF16).T
    wait_all(l_relay)
    for j in range(4):
        projected = tdot(rl[...].reshape(2048, 256), tl[j]).astype(BF16)
        cm = dot(coup[j], projected)
        keep = lax.broadcasted_iota(jnp.int32, (256, 256), 1) < rank_n[0, j]
        comb[j] = jnp.where(keep, cm, 0.0).astype(BF16)

    def update(i, j):
        second = dot(cl[j, i].reshape(512, 256), comb[j])
        out[0, j, chip_rows(i), :] = (term[j, i] - second).astype(BF16)

    for j in range(4):
        panel_far(1, j)
        panel_sibling(1, j, (OWN_SIB, BACK_SIB, AHEAD_SIB))
        for i in range(3):
            update(i, j)
    for j in range(4):
        panel_sibling(1, j, (FAR_SIB,))
        update(3, j)

    for p in range(4):

        @pl.when(x == p)
        def _():
            for n in range(3):
                part = dm.at[p, k, z, y, :, pl.ds(0, 512 * (p + 1))]
                remote("diag", part, part, d_send.at[n], d_recv.at[p], far).wait_send()

    for copy in pending:
        copy.wait_send()
    for t in range(2):
        for j in range(4):
            for kind in range(7):
                panel_copy(kind, t, j).wait_send()


def on_device(
    diag_inverse, row_left, row_right, col_left, col_right, row_ranks, col_ranks, tile_left, tile_right, new_ranks
):
    hbm = pl.BlockSpec(memory_space=pltpu.HBM)
    operands = (
        col_ranks, new_ranks, diag_inverse, row_left, row_right, col_left, col_right, tile_left, tile_right
    )
    dma = pltpu.SemaphoreType.DMA
    return pl.pallas_call(
        kernel,
        out_shape=pltpu.VMEM(tile_right.shape, tile_right.dtype),
        in_specs=[pl.BlockSpec(memory_space=pltpu.SMEM)] + [hbm] * 9,
        out_specs=pl.BlockSpec(memory_space=pltpu.VMEM),
        scratch_shapes=[
            pltpu.VMEM((4, 2048, 256), BF16),
            pltpu.VMEM((4, 2048, 256), BF16),
            pltpu.VMEM((4, 8, 256, 256), BF16),
            pltpu.VMEM((4, 4, 2, 256, 256), BF16),
            pltpu.VMEM((4, 4, 128, 256), BF16),
            pltpu.VMEM((4, 4, 128, 256), BF16),
            pltpu.VMEM((256, 1536), F32),
            pltpu.VMEM((256, 2048), BF16),
            pltpu.VMEM((4, 2, 4, 4, 16, 2048), BF16),
            pltpu.VMEM((4, 256, 256), BF16),
            pltpu.VMEM((4, 256, 256), BF16),
            pltpu.VMEM((4, 256, 256), BF16),
            pltpu.VMEM((4, 4, 512, 256), F32),
            pltpu.SMEM((4,), jnp.int32),
            pltpu.SMEM((1, 4), jnp.int32),
            dma((12,)),
            dma((7, 8)),
            dma((7, 8)),
            dma((3,)),
            dma((4,)),
            dma((4,)),
            dma((4,)),
            dma((6, 18)),
            dma((6, 18)),
        ],
        compiler_params=pltpu.CompilerParams(
            collective_id=0, has_side_effects=True, vmem_limit_bytes=52 * 1024 * 1024
        ),
        name="panel_step",
    )(row_ranks, *[pltpu.with_memory_space_constraint(a, pltpu.HBM) for a in operands])


def solution(mesh):
    in_specs = (
        P(("row", "col"), None),
        P("row", "col", None),
        P("row", "col", None),
        P("col", "row", None),
        P("col", "row", None),
        P("row"),
        P("col"),
        P("row", "col", None, None),
        P("row", "col", None, None),
        P("row", "col"),
    )
    out_specs = P("row", "col", None, None)
    return jax.shard_map(on_device, mesh=mesh, in_specs=in_specs, out_specs=out_specs, check_vma=False)
```

time: 68.1 us -> 57.5 us (0.84)
  Pallas kernels: 62.8 us -> 54.7 us
  local copies, waits for them, and re-layouts: 4.47 us -> 2.02 us
    pallas_call x1, Pallas kernels: 62.8 us -> 54.7 us  [on_device(): pl.pallas_call(kernel, out_shape=pltpu.VMEM(tile_right.shape, tile_right....]
    unnamed x1, local copies, waits for them, and re-layouts: 4.47 us -> 2.02 us
where the time goes in v2:
time: 57.5 us; the launch traced here: 57.4 us
  Pallas kernels  54.7 us (95%)
  local copies, waits for them, and re-layouts  2.02 us (4%)
  between operations  0.66 us (1%)
    pallas_call x1, Pallas kernels, on_device(): pl.pallas_call(kernel, out_shape=pltpu.VMEM(tile_right.shape, tile_right....  54.7 us
    unnamed x1, local copies, waits for them, and re-layouts  2.02 us

profile of v2, /device:TPU:1, one launch (start us, length us, event | category | flops | bytes accessed | tf_op | source)
XLA Modules:
  0.0 57.4 jit_solution(688741965367328769)
XLA Ops:
  0.7 54.7 %panel_step.1 = bf16[1,4,2048,256]{3,2,1,0:T(8,128)(2,1)S(1)} custom-call(s32[1]{0:T(128)S(6)} %copy.13.row_ranks, s32[4]{0:T(128)} %col_ranks.1, s32[1,4]{1,0:T(1,128)} %new_ranks.1, bf16[16,2048]{1,0:T(8,128)(2,1)} %diag.1, bf16[1,128,256]{2,1,0:T(8,128)(2,1)} %row_left.1, bf16[1,128,256]{2,1,0:T(8,128)(2,1)} %row_right.1, bf16[4,256,256]{2,1,0:T(8,128)(2,1)} %col_left.1, ...), custom_call_target="tpu_custom_call" | custom-call | tf_op jit(solution)/shard_map/panel_step/pallas_call | solution.py:356
  55.3 2.0 %copy.12 = bf16[1,4,2048,256]{3,2,1,0:T(8,128)(2,1)} copy(bf16[1,4,2048,256]{3,2,1,0:T(8,128)(2,1)S(1)} %panel_step.1) | data formatting | bytes 8388608

commit v3 on v2

--- a/solution.py
+++ b/solution.py
@@ -46,7 +46,7 @@
     cl,
     rl,
     xr,
-    yacc,
+    st,
     yt,
     dm,
     gram,
@@ -225,19 +225,15 @@
         pending.append(copy)
         return copy
 
-    def solve(p):
+    def solve(p, q):
         width = 512 * (p + 1)
-        a = dm[p, :, :, :, :, 0:width].reshape(512, width)
-        solved = dot(a, xr[0 : p + 1].reshape(width, 256)).astype(BF16).T
-        for b in range(p + 1):
-            cols = slice(512 * b, 512 * b + 512)
-            acc = dot(solved, dm[p, :, :, :, :, cols].reshape(512, 512))
-            if p < 3:
-                acc += yacc[:, cols]
-            if b == p:
-                yt[:, cols] = acc.astype(BF16)
-            else:
-                yacc[:, cols] = acc
+        solved = dot(dm[p, q, :, :, :, 0:width].reshape(256, width), xr[0 : p + 1].reshape(width, 256))
+        st[p, q] = solved.astype(BF16).T
+
+    def solve_back(p):
+        rows = jnp.concatenate([st[m, q] for m in range(p, 4) for q in range(2)], axis=1)
+        block = dm[p:4, :, :, :, :, 512 * p : 512 * p + 512].reshape(512 * (4 - p), 512)
+        yt[:, 512 * p : 512 * p + 512] = dot(rows, block).astype(BF16)
 
     chips = (x, (x + 1) % 4, (x + 3) % 4, far_x)
 
@@ -267,10 +263,10 @@
     panel_pass(0, 0)
     local_products(2)
     x_relay = gather_relay(0, x_view, x_second)
+    for p in (3, 2, 1, 0):
+        d_second[p] = gather_second(2 + p, d_view[p], d_first[p])
     panel_pass(0, 1)
     local_products(3)
-    for p in (3, 2, 1, 0):
-        d_second[p] = gather_second(2 + p, d_view[p], d_first[p])
     load_tr.wait()
     first_term(0)
     panel_pass(0, 2)
@@ -279,26 +275,29 @@
     panel_pass(0, 3)
     first_term(3)
     wait_all(x_relay)
+    for p in (3, 2, 1, 0):
+        d_relay[p] = gather_relay(2 + p, d_view[p], d_second[p])
     panel_pass(1, 0)
-    d_relay[3] = gather_relay(5, d_view[3], d_second[3])
+    shares = {3: diag_share(3)}
+    solve(3, k)
     panel_pass(1, 1)
-    for p in (2, 1, 0):
-        d_relay[p] = gather_relay(2 + p, d_view[p], d_second[p])
+    shares[2] = diag_share(2)
     load_l.wait()
     l_second = gather_second(1, l_view, l_first)
+    solve(2, k)
     panel_pass(1, 2)
-    shares = {3: diag_share(3)}
+    shares.update({p: diag_share(p) for p in (1, 0)})
+    for p in (3, 2):
+        shares[p].wait_recv()
+        solve(p, 1 - k)
+        solve_back(p)
     panel_pass(1, 3)
-    shares[2] = diag_share(2)
-    shares[3].wait_recv()
-    solve(3)
-    shares.update({p: diag_share(p) for p in (1, 0)})
-    shares[2].wait_recv()
-    solve(2)
     l_relay = gather_relay(1, l_view, l_second)
     for p in (1, 0):
+        solve(p, k)
         shares[p].wait_recv()
-        solve(p)
+        solve(p, 1 - k)
+        solve_back(p)
     for j in range(4):
         panel_far(0, j)
 
@@ -365,7 +364,7 @@
             pltpu.VMEM((4, 4, 2, 256, 256), BF16),
             pltpu.VMEM((4, 4, 128, 256), BF16),
             pltpu.VMEM((4, 4, 128, 256), BF16),
-            pltpu.VMEM((256, 1536), F32),
+            pltpu.VMEM((4, 2, 256, 256), BF16),
             pltpu.VMEM((256, 2048), BF16),
             pltpu.VMEM((4, 2, 4, 4, 16, 2048), BF16),
             pltpu.VMEM((4, 256, 256), BF16),

time: 57.5 us -> 54.7 us (0.951)
  Pallas kernels: 54.7 us -> 51.9 us
    pallas_call x1, Pallas kernels: 54.7 us -> 51.9 us  [on_device(): pl.pallas_call(kernel, out_shape=pltpu.VMEM(tile_right.shape, tile_right....]
where the time goes in v3:
time: 54.7 us; the launch traced here: 54.6 us
  Pallas kernels  51.9 us (95%)
  local copies, waits for them, and re-layouts  2.02 us (4%)
  between operations  0.66 us (1%)
    pallas_call x1, Pallas kernels, on_device(): pl.pallas_call(kernel, out_shape=pltpu.VMEM(tile_right.shape, tile_right....  51.9 us
    unnamed x1, local copies, waits for them, and re-layouts  2.02 us

profile of v3, /device:TPU:1, one launch (start us, length us, event | category | flops | bytes accessed | tf_op | source)
XLA Modules:
  0.0 54.6 jit_solution(14714074363275659999)
XLA Ops:
  0.7 51.9 %panel_step.1 = bf16[1,4,2048,256]{3,2,1,0:T(8,128)(2,1)S(1)} custom-call(s32[1]{0:T(128)S(6)} %copy.13.row_ranks, s32[4]{0:T(128)} %col_ranks.1, s32[1,4]{1,0:T(1,128)} %new_ranks.1, bf16[16,2048]{1,0:T(8,128)(2,1)} %diag.1, bf16[1,128,256]{2,1,0:T(8,128)(2,1)} %row_left.1, bf16[1,128,256]{2,1,0:T(8,128)(2,1)} %row_right.1, bf16[4,256,256]{2,1,0:T(8,128)(2,1)} %col_left.1, ...), custom_call_target="tpu_custom_call" | custom-call | tf_op jit(solution)/shard_map/panel_step/pallas_call | solution.py:355
  52.6 2.0 %copy.12 = bf16[1,4,2048,256]{3,2,1,0:T(8,128)(2,1)} copy(bf16[1,4,2048,256]{3,2,1,0:T(8,128)(2,1)S(1)} %panel_step.1) | data formatting | bytes 8388608

commit v4 on v3

--- a/solution.py
+++ b/solution.py
@@ -50,7 +50,7 @@
     yt,
     dm,
     gram,
-    coup,
+    proj,
     comb,
     term,
     rank_c,
@@ -129,6 +129,17 @@
                     pending.append(copy)
         return halves
 
+    def gather_direct(n, view, firsts):
+        wait_all(firsts)
+        copies = []
+        for d in (1, 3, 2):
+            for h, device in ((0, (r, 4 * ((z + d) % 4) + y)), (1, (r, 4 * z + (y + d) % 4))):
+                part = view(0, z, slice(None)) if h == 0 else view(1, slice(None), y)
+                s = 6 + 3 * h + d - 1
+                copies.append(send("gather", part, part, g_send.at[n, s], g_recv.at[n, s], device))
+        pending.extend(copies)
+        return copies
+
     def gather_relay(n, view, halves):
         copies = []
         for copy, h, e, d, half in halves:
@@ -229,6 +240,13 @@
         width = 512 * (p + 1)
         solved = dot(dm[p, q, :, :, :, 0:width].reshape(256, width), xr[0 : p + 1].reshape(width, 256))
         st[p, q] = solved.astype(BF16).T
+
+    def solve_both(p):
+        width = 512 * (p + 1)
+        solved = dot(dm[p, :, :, :, :, 0:width].reshape(512, width), xr[0 : p + 1].reshape(width, 256))
+        solved = solved.astype(BF16)
+        for q in range(2):
+            st[p, q] = solved[256 * q : 256 * q + 256].T
 
     def solve_back(p):
         rows = jnp.concatenate([st[m, q] for m in range(p, 4) for q in range(2)], axis=1)
@@ -277,13 +295,13 @@
     wait_all(x_relay)
     for p in (3, 2, 1, 0):
         d_relay[p] = gather_relay(2 + p, d_view[p], d_second[p])
+    load_l.wait()
+    l_second = gather_direct(1, l_view, l_first)
     panel_pass(1, 0)
     shares = {3: diag_share(3)}
     solve(3, k)
     panel_pass(1, 1)
     shares[2] = diag_share(2)
-    load_l.wait()
-    l_second = gather_second(1, l_view, l_first)
     solve(2, k)
     panel_pass(1, 2)
     shares.update({p: diag_share(p) for p in (1, 0)})
@@ -292,26 +310,25 @@
         solve(p, 1 - k)
         solve_back(p)
     panel_pass(1, 3)
-    l_relay = gather_relay(1, l_view, l_second)
     for p in (1, 0):
-        solve(p, k)
         shares[p].wait_recv()
-        solve(p, 1 - k)
+        solve_both(p)
         solve_back(p)
-    for j in range(4):
-        panel_far(0, j)
-
+    panel_far(0, 0)
+
+    wait_all(l_second)
+    for j in range(4):
+        proj[j] = tdot(rl[...].reshape(2048, 256), tl[j]).astype(BF16)
+        if j < 3:
+            panel_far(0, j + 1)
     for j in range(4):
         panel_sibling(0, j, (OWN_SIB, BACK_SIB, AHEAD_SIB, FAR_SIB))
         g = dot(yt[...], cr[j].reshape(2048, 256))
         keep = (lax.broadcasted_iota(jnp.int32, (256, 256), 0) < row_ranks[0]) & (
             lax.broadcasted_iota(jnp.int32, (256, 256), 1) < rank_c[j]
         )
-        coup[j] = jnp.where(keep, g, 0.0).astype(BF16).T
-    wait_all(l_relay)
-    for j in range(4):
-        projected = tdot(rl[...].reshape(2048, 256), tl[j]).astype(BF16)
-        cm = dot(coup[j], projected)
+        coupling = jnp.where(keep, g, 0.0).astype(BF16)
+        cm = tdot(coupling, proj[j])
         keep = lax.broadcasted_iota(jnp.int32, (256, 256), 1) < rank_n[0, j]
         comb[j] = jnp.where(keep, cm, 0.0).astype(BF16)
 

time: 54.7 us -> 54.3 us (level)
  no operation moved by 1% of the time
where the time goes in v4:
time: 54.3 us; the launch traced here: 54.2 us
  Pallas kernels  51.5 us (95%)
  local copies, waits for them, and re-layouts  2.02 us (4%)
  between operations  0.66 us (1%)
    pallas_call x1, Pallas kernels, on_device(): pl.pallas_call(kernel, out_shape=pltpu.VMEM(tile_right.shape, tile_right....  51.5 us
    unnamed x1, local copies, waits for them, and re-layouts  2.02 us

profile of v4, /device:TPU:1, one launch (start us, length us, event | category | flops | bytes accessed | tf_op | source)
XLA Modules:
  0.0 54.2 jit_solution(16398970738251115412)
XLA Ops:
  0.7 51.5 %panel_step.1 = bf16[1,4,2048,256]{3,2,1,0:T(8,128)(2,1)S(1)} custom-call(s32[1]{0:T(128)S(6)} %copy.13.row_ranks, s32[4]{0:T(128)} %col_ranks.1, s32[1,4]{1,0:T(1,128)} %new_ranks.1, bf16[16,2048]{1,0:T(8,128)(2,1)} %diag.1, bf16[1,128,256]{2,1,0:T(8,128)(2,1)} %row_left.1, bf16[1,128,256]{2,1,0:T(8,128)(2,1)} %row_right.1, bf16[4,256,256]{2,1,0:T(8,128)(2,1)} %col_left.1, ...), custom_call_target="tpu_custom_call" | custom-call | tf_op jit(solution)/shard_map/panel_step/pallas_call | solution.py:372
  52.2 2.0 %copy.12 = bf16[1,4,2048,256]{3,2,1,0:T(8,128)(2,1)} copy(bf16[1,4,2048,256]{3,2,1,0:T(8,128)(2,1)S(1)} %panel_step.1) | data formatting | bytes 8388608

commit v5 on v4

--- a/solution.py
+++ b/solution.py
@@ -300,27 +300,24 @@
     panel_pass(1, 0)
     shares = {3: diag_share(3)}
     solve(3, k)
-    panel_pass(1, 1)
     shares[2] = diag_share(2)
     solve(2, k)
-    panel_pass(1, 2)
+    panel_pass(1, 1)
     shares.update({p: diag_share(p) for p in (1, 0)})
     for p in (3, 2):
         shares[p].wait_recv()
         solve(p, 1 - k)
         solve_back(p)
-    panel_pass(1, 3)
+        panel_pass(1, 5 - p)
     for p in (1, 0):
         shares[p].wait_recv()
         solve_both(p)
         solve_back(p)
-    panel_far(0, 0)
 
     wait_all(l_second)
     for j in range(4):
         proj[j] = tdot(rl[...].reshape(2048, 256), tl[j]).astype(BF16)
-        if j < 3:
-            panel_far(0, j + 1)
+        panel_far(0, j)
     for j in range(4):
         panel_sibling(0, j, (OWN_SIB, BACK_SIB, AHEAD_SIB, FAR_SIB))
         g = dot(yt[...], cr[j].reshape(2048, 256))

time: 54.3 us -> 53.9 us (level)
  no operation moved by 1% of the time
where the time goes in v5:
time: 53.9 us; the launch traced here: 53.8 us
  Pallas kernels  51.1 us (95%)
  local copies, waits for them, and re-layouts  2.02 us (4%)
  between operations  0.66 us (1%)
    pallas_call x1, Pallas kernels, on_device(): pl.pallas_call(kernel, out_shape=pltpu.VMEM(tile_right.shape, tile_right....  51.1 us
    unnamed x1, local copies, waits for them, and re-layouts  2.02 us

profile of v5, /device:TPU:1, one launch (start us, length us, event | category | flops | bytes accessed | tf_op | source)
XLA Modules:
  0.0 53.8 jit_solution(6646965411248421744)
XLA Ops:
  0.7 51.1 %panel_step.1 = bf16[1,4,2048,256]{3,2,1,0:T(8,128)(2,1)S(1)} custom-call(s32[1]{0:T(128)S(6)} %copy.13.row_ranks, s32[4]{0:T(128)} %col_ranks.1, s32[1,4]{1,0:T(1,128)} %new_ranks.1, bf16[16,2048]{1,0:T(8,128)(2,1)} %diag.1, bf16[1,128,256]{2,1,0:T(8,128)(2,1)} %row_left.1, bf16[1,128,256]{2,1,0:T(8,128)(2,1)} %row_right.1, bf16[4,256,256]{2,1,0:T(8,128)(2,1)} %col_left.1, ...), custom_call_target="tpu_custom_call" | custom-call | tf_op jit(solution)/shard_map/panel_step/pallas_call | solution.py:369
  51.8 2.0 %copy.12 = bf16[1,4,2048,256]{3,2,1,0:T(8,128)(2,1)} copy(bf16[1,4,2048,256]{3,2,1,0:T(8,128)(2,1)S(1)} %panel_step.1) | data formatting | bytes 8388608

commit v6 on v5

--- a/solution.py
+++ b/solution.py
@@ -96,13 +96,13 @@
         copy.start()
         return copy
 
-    load_ranks = [load(col_ranks, rank_c, 10), load(new_ranks, rank_n, 11)]
     load_x = load(row_right.at[0], xr.at[z, y], 1)
     load_d = load(diag, dm.at[x, k, z, y], 0)
-    load_tl = [load(tile_left.at[0, j], tl.at[j], 3 + j) for j in range(4)]
     load_l = load(row_left.at[0], rl.at[z, y], 2)
     load_cr = load(col_right, cr.at[:, r], 7)
     load_cl = load(col_left, cl.at[:, 0, k], 8)
+    load_tl = [load(tile_left.at[0, j], tl.at[j], 3 + j) for j in range(4)]
+    load_ranks = [load(col_ranks, rank_c, 10), load(new_ranks, rank_n, 11)]
     load_tr = load(tile_right.at[0], tr, 9)
     pl.semaphore_wait(barrier, 10)
 
@@ -173,7 +173,7 @@
     ahead_slot = 2 * ahead_x + k
     far_slot = 2 * far_x + k
 
-    def panel_copy(kind, t, j):
+    def panel_copy(kind, t, j, own=None):
         if t == 0:
             slot = {PASS_AHEAD: back_slot, BACK_SIB: back_slot, AHEAD_SIB: ahead_slot, FAR_SIB: far_slot}.get(kind, r)
             src = dst = cr.at[j, slot]
@@ -183,11 +183,14 @@
             src, dst = cl.at[j, here, k], cl.at[j, there, k]
         device = {OWN_AHEAD: ahead, PASS_AHEAD: ahead, OWN_BACK: back}.get(kind, sib)
         s = 4 * t + j
+        src = src if own is None else own
         return remote("panel", src, dst, x_send.at[kind, s], x_recv.at[kind, s], device)
+
+    sources = (col_right, col_left)
 
     def panel_own(t, j):
         for kind in (OWN_AHEAD, OWN_BACK, OWN_SIB):
-            panel_copy(kind, t, j).start()
+            panel_copy(kind, t, j, sources[t].at[j]).start()
 
     def panel_pass(t, j):
         panel_copy(OWN_AHEAD, t, j).wait_recv()
@@ -216,8 +219,6 @@
     d_view = [diag_view(p) for p in range(4)]
     x_first = gather_first(0, [row_right.at[0, pl.ds(64 * h, 64)] for h in range(2)], x_view)
     l_first = gather_first(1, [row_left.at[0, pl.ds(64 * h, 64)] for h in range(2)], l_view)
-    load_cr.wait()
-    load_cl.wait()
     for j in range(4):
         panel_own(0, j)
     for j in range(4):
@@ -285,6 +286,8 @@
         d_second[p] = gather_second(2 + p, d_view[p], d_first[p])
     panel_pass(0, 1)
     local_products(3)
+    load_cr.wait()
+    load_cl.wait()
     load_tr.wait()
     first_term(0)
     panel_pass(0, 2)

time: 53.9 us -> 54.2 us (level)
  no operation moved by 1% of the time
where the time goes in v6:
time: 54.2 us; the launch traced here: 54 us
  Pallas kernels  51.4 us (95%)
  local copies, waits for them, and re-layouts  2.02 us (4%)
  between operations  0.66 us (1%)
    pallas_call x1, Pallas kernels, on_device(): pl.pallas_call(kernel, out_shape=pltpu.VMEM(tile_right.shape, tile_right....  51.4 us
    unnamed x1, local copies, waits for them, and re-layouts  2.02 us

profile of v6, /device:TPU:1, one launch (start us, length us, event | category | flops | bytes accessed | tf_op | source)
XLA Modules:
  0.0 54.0 jit_solution(12543304005661313357)
XLA Ops:
  0.7 51.4 %panel_step.1 = bf16[1,4,2048,256]{3,2,1,0:T(8,128)(2,1)S(1)} custom-call(s32[1]{0:T(128)S(6)} %copy.13.row_ranks, s32[4]{0:T(128)} %col_ranks.1, s32[1,4]{1,0:T(1,128)} %new_ranks.1, bf16[16,2048]{1,0:T(8,128)(2,1)} %diag.1, bf16[1,128,256]{2,1,0:T(8,128)(2,1)} %row_left.1, bf16[1,128,256]{2,1,0:T(8,128)(2,1)} %row_right.1, bf16[4,256,256]{2,1,0:T(8,128)(2,1)} %col_left.1, ...), custom_call_target="tpu_custom_call" | custom-call | tf_op jit(solution)/shard_map/panel_step/pallas_call | solution.py:372
  52.0 2.0 %copy.12 = bf16[1,4,2048,256]{3,2,1,0:T(8,128)(2,1)} copy(bf16[1,4,2048,256]{3,2,1,0:T(8,128)(2,1)S(1)} %panel_step.1) | data formatting | bytes 8388608
